TPU v7x, 512 devices: a whole 4x4x16 slice. The times are simulated.
512 devices in a mesh: batch: 32 (over y, x, core), proto: 16 (over z).
Axes of the slice: x: 4, y: 4, z: 16, core: 2. Of those that a mesh axis runs over, the one named last changes fastest.
Arguments:
- teacher_feat: bfloat16 [4096, 256], P('batch'), may hold values from -12 to 12
- student_feat: bfloat16 [4096, 256], P('batch'), may hold values from -48 to 48
- teacher_proto: bfloat16 [131072, 256], P(('proto', 'batch')), may hold values from -2 to 2
- student_proto: bfloat16 [131072, 256], P(('proto', 'batch')), may hold values from -0.375 to 0.375
Outputs:
- targets: bfloat16 [4096, 131072], P('batch', 'proto')
- student_grad: float32 [4096, 256], P('batch')
- loss: float32 [], replicated
All inputs are finite; a program needn't handle non-finite values.
Results may differ from a plain program's by a relative error of at most 0.004.
Values may be sent and summed in bfloat16 or wider, within the bound.
A program may use at most 128 MiB of HBM per device.

v0:
```python
import jax
import jax.numpy as jnp
from jax import lax
from jax.sharding import PartitionSpec as P

PROTOS = 131072
ITERS = 3


teacher_temp = 0.07
student_temp = 0.1


def merged(part, axis, combine):
    gathered = jax.tree.map(lambda a: lax.all_gather(a, axis), part)

    def take(source):
        return jax.tree.map(lambda a: lax.dynamic_index_in_dim(a, source, 0, False), gathered)

    return lax.fori_loop(
        1, lax.axis_size(axis), lambda source, state: combine(state, take(source)), take(0)
    )


def map_against_centers(embedding_lines, center_lines, sharpening_divisor):
    return (
        lax.dot_general(
            embedding_lines,
            center_lines,
            (((1,), (1,)), ((), ())),
            preferred_element_type=jnp.float32,
        )
        / sharpening_divisor
    )


def combine_stats(first_pair, second_pair):
    highest_value = jnp.maximum(first_pair[0], second_pair[0])
    summed = first_pair[1] * jnp.exp(first_pair[0] - highest_value) + second_pair[1] * jnp.exp(
        second_pair[0] - highest_value
    )
    return (highest_value, summed)


def on_device(teacher_feat, student_feat, teacher_proto, student_proto):
    row_dev = teacher_feat.shape[0]
    total_rows = row_dev * lax.axis_size("batch")
    teach_all, stud_all = (
        lax.all_gather(teacher_proto, "batch", axis=0, tiled=True),
        lax.all_gather(student_proto, "batch", axis=0, tiled=True),
    )
    proto_cols = teach_all.shape[0]
    block_cols = min(1024, proto_cols)
    block_count = proto_cols // block_cols
    scores = map_against_centers(teacher_feat, teach_all, teacher_temp)
    colmax = lax.pmax(jnp.max(scores, axis=0).astype(jnp.bfloat16), "batch").astype(jnp.float32)

    def stat_pass(block_index, carried):
        logit_max, logit_sum = carried
        center_lines = lax.dynamic_slice_in_dim(stud_all, block_index * block_cols, block_cols, 0)
        logits = map_against_centers(student_feat, center_lines, student_temp)
        highest_logit = jnp.maximum(logit_max, jnp.max(logits, axis=1))
        logit_sum = logit_sum * jnp.exp(logit_max - highest_logit) + jnp.sum(
            jnp.exp(logits - highest_logit[:, None]), axis=1
        )
        return (highest_logit, logit_sum)

    start_state = (jnp.full((row_dev,), -jnp.inf, jnp.float32), jnp.zeros((row_dev,), jnp.float32))
    logit_max, logit_sum = lax.fori_loop(0, block_count, stat_pass, start_state)
    logit_max, logit_sum = merged((logit_max, logit_sum), "proto", combine_stats)
    kernel = jnp.exp(scores - colmax[None, :])
    weight_rows = jnp.ones((row_dev,), jnp.float32)
    col_scale = jnp.ones((proto_cols,), jnp.float32)
    for sweep_step in range(ITERS):
        colsum = jnp.dot(weight_rows, kernel, precision=lax.Precision.HIGHEST)
        colsum = lax.psum(colsum, "batch")
        col_scale = 1.0 / (PROTOS * colsum)
        rowsum = jnp.dot(kernel, col_scale, precision=lax.Precision.HIGHEST)
        rowsum = lax.psum(rowsum, "proto")
        weight_rows = 1.0 / (total_rows * rowsum)
    log_norm = logit_max + jnp.log(logit_sum)

    def last_pass(block_index, carried):
        targets, grad_part, loss_part = carried
        col_factor = lax.dynamic_slice_in_dim(col_scale, block_index * block_cols, block_cols, 0)
        kernel_cols = lax.dynamic_slice_in_dim(kernel, block_index * block_cols, block_cols, 1)
        plan = total_rows * weight_rows[:, None] * kernel_cols * col_factor[None, :]
        center_lines = lax.dynamic_slice_in_dim(stud_all, block_index * block_cols, block_cols, 0)
        log_probs = (
            map_against_centers(student_feat, center_lines, student_temp) - log_norm[:, None]
        )
        loss_part = loss_part - jnp.sum(plan * log_probs)
        logit_grad = ((jnp.exp(log_probs) - plan) / (total_rows * student_temp)).astype(
            jnp.bfloat16
        )
        grad_part = grad_part + jnp.dot(
            logit_grad, center_lines, preferred_element_type=jnp.float32
        )
        targets = lax.dynamic_update_slice_in_dim(
            targets, plan.astype(jnp.bfloat16), block_index * block_cols, 1
        )
        return (targets, grad_part, loss_part)

    start_final = (
        jnp.zeros((row_dev, proto_cols), jnp.bfloat16),
        jnp.zeros((row_dev, teacher_feat.shape[1]), jnp.float32),
        jnp.zeros((), jnp.float32),
    )
    targets, grad_part, loss_part = lax.fori_loop(0, block_count, last_pass, start_final)
    student_grad = lax.psum(grad_part, "proto")
    loss_value = lax.psum(loss_part, ("batch", "proto")) / total_rows
    return (targets, student_grad, loss_value)


def solution(mesh):
    return jax.shard_map(
        on_device,
        mesh=mesh,
        in_specs=(
            P("batch", None),
            P("batch", None),
            P(("proto", "batch"), None),
            P(("proto", "batch"), None),
        ),
        out_specs=(P("batch", "proto"), P("batch", None), P()),
        check_vma=False,
    )
```

profile of v0, /device:TPU:6, one launch (start us, length us, event | category | flops | bytes accessed | tf_op | source)
XLA Modules:
  0.0 952.5 jit_solution(5335446070049559657)
XLA Ops:
  8.7 67.9 %all-gather.9.cloned.1.call-done = bf16[8192,256]{1,0:T(8,128)(2,1)} async-done(((bf16[256,256]{1,0:T(8,128)(2,1)}), bf16[8192,256]{1,0:T(8,128)(2,1)}) %all-gather.9.cloned.1.call-update) | async-done | bytes 4194320 | tf_op jit(solution)/shard_map/all_gather | solution.py:50
  76.6 12.8 %while.52 = (s32[]{:T(128)}, f32[128]{0:T(128)S(1)}, f32[128]{0:T(128)S(1)}, bf16[8192,256]{1,0:T(8,128)(2,1)}, bf16[128,256]{1,0:T(8,128)(2,1)}, /*index=5*/s32[]{:T(128)}, s32[]{:T(128)}, s32[]{:T(128)}, s32[]{:T(128)}) while((s32[]{:T(128)}, f32[128]{0:T(128)S(1)}, f32[128]{0:T(128)S(1)}, bf16[8192,256]{1,0:T(8,128)(2,1)}, ...), condition=%wide.region_11.12_spmd.clone, body=%wide.region_8.11_spmd.clone.sunk | while | flops 67633800 | bytes 1645218 | solution.py:69
  78.2 1.4 fusion.61
  79.8 1.4 fusion.61
  81.4 1.4 fusion.61
  83.1 1.4 fusion.61
  84.7 1.4 fusion.61
  86.3 1.4 fusion.61
  87.9 1.4 fusion.61
  89.5 30.0 %all-gather.2 = f32[16,1,128]{2,1,0:T(1,128)S(1)} all-gather(f32[1,1,128]{2,1,0:T(1,128)S(1)} %bitcast.65), channel_id=2, replica_groups=mesh['batch'=32,'proto'=16] {'proto'}, dimensions={0}, use_global_device_ids=true | all-gather | bytes 8704 | tf_op jit(solution)/shard_map/all_gather | solution.py:15
  119.4 27.1 %all-gather.3 = f32[16,1,128]{2,1,0:T(1,128)S(1)} all-gather(f32[1,1,128]{2,1,0:T(1,128)S(1)} %bitcast.66), channel_id=3, replica_groups=mesh['batch'=32,'proto'=16] {'proto'}, dimensions={0}, use_global_device_ids=true | all-gather | bytes 8704 | tf_op jit(solution)/shard_map/all_gather | solution.py:15
  147.2 5.7 fusion.38
  152.9 109.4 %pmax.7 = bf16[8192]{0:T(1024)(128)(2,1)S(1)} all-reduce(bf16[8192]{0:T(1024)(128)(2,1)S(1)} %get-tuple-element.533), channel_id=1, replica_groups=mesh['batch'=32,'proto'=16] {'batch'}, use_global_device_ids=true, to_apply=%region_1.0 | all-reduce | flops 8192 | bytes 32768 | tf_op jit(solution)/shard_map/pmax | solution.py:56
  262.3 2.7 subtract_exponential_fusion
  265.0 2.0 copy-done.1
  267.0 2.1 fusion.26
  269.1 123.8 %psum.56 = f32[8192]{0:T(1024)S(1)} all-reduce(f32[8192]{0:T(1024)S(1)} %bitcast.64), channel_id=1, replica_groups=mesh['batch'=32,'proto'=16] {'batch'}, use_global_device_ids=true, to_apply=%region_2.3 | all-reduce | flops 8192 | bytes 65536 | tf_op jit(solution)/shard_map/psum | solution.py:76
  392.9 5.1 convolution_bitcast_fusion.2
  397.9 28.9 %psum.57 = f32[128]{0:T(128)S(1)} all-reduce(f32[128]{0:T(128)S(1)} %convolution_bitcast_fusion.2), channel_id=1, replica_groups=mesh['batch'=32,'proto'=16] {'proto'}, use_global_device_ids=true, to_apply=%region_3.4 | all-reduce | flops 128 | bytes 1024 | tf_op jit(solution)/shard_map/psum | solution.py:79
  426.8 4.3 fusion.20
  431.0 123.8 %psum.58 = f32[8192]{0:T(1024)S(1)} all-reduce(f32[8192]{0:T(1024)S(1)} %bitcast.61), channel_id=1, replica_groups=mesh['batch'=32,'proto'=16] {'batch'}, use_global_device_ids=true, to_apply=%region_4.5 | all-reduce | flops 8192 | bytes 65536 | tf_op jit(solution)/shard_map/psum | solution.py:76
  554.8 5.1 convolution_bitcast_fusion.1
  559.9 28.1 %psum.59 = f32[128]{0:T(128)S(1)} all-reduce(f32[128]{0:T(128)S(1)} %convolution_bitcast_fusion.1), channel_id=1, replica_groups=mesh['batch'=32,'proto'=16] {'proto'}, use_global_device_ids=true, to_apply=%region_5.0 | all-reduce | flops 128 | bytes 1024 | tf_op jit(solution)/shard_map/psum | solution.py:79
  588.0 4.3 fusion.18
  592.2 123.9 %psum.60 = f32[8192]{0:T(1024)S(1)} all-reduce(f32[8192]{0:T(1024)S(1)} %bitcast.63), channel_id=1, replica_groups=mesh['batch'=32,'proto'=16] {'batch'}, use_global_device_ids=true, to_apply=%region_6.7 | all-reduce | flops 8192 | bytes 65536 | tf_op jit(solution)/shard_map/psum | solution.py:76
  716.1 5.1 convolution_bitcast_fusion
  721.2 28.1 %psum.61 = f32[128]{0:T(128)S(1)} all-reduce(f32[128]{0:T(128)S(1)} %convolution_bitcast_fusion), channel_id=1, replica_groups=mesh['batch'=32,'proto'=16] {'proto'}, use_global_device_ids=true, to_apply=%region_7.8 | all-reduce | flops 128 | bytes 1024 | tf_op jit(solution)/shard_map/psum | solution.py:79
  749.4 1.5 broadcast_in_dim.25.clone
  750.9 50.9 %while.53 = (s32[]{:T(128)}, bf16[128,8192]{1,0:T(8,128)(2,1)}, f32[128,256]{1,0:T(8,128)S(1)}, f32[]{:T(128)}, f32[128]{0:T(128)S(1)}, /*index=5*/f32[128,8192]...) while((s32[]{:T(128)}, bf16[128,8192]{1,0:T(8,128)(2,1)}, ...), condition=%wide.region_16.17_spmd.clone, body=%wide.region_14.16_spmd.clone.sunk | while | flops 135856256 | bytes 6900457 | solution.py:109
  752.2 2.0 multiply_reduce_fusion.2
  754.9 1.5 convolution_add_fusion.2
  758.5 2.0 multiply_reduce_fusion.2
  761.2 1.5 convolution_add_fusion.2
  764.9 2.0 multiply_reduce_fusion.2
  767.6 1.5 convolution_add_fusion.2
  771.3 2.0 multiply_reduce_fusion.2
  773.9 1.5 convolution_add_fusion.2
  777.6 2.0 multiply_reduce_fusion.2
  780.3 1.5 convolution_add_fusion.2
  784.0 2.0 multiply_reduce_fusion.2
  786.7 1.5 convolution_add_fusion.2
  790.3 2.0 multiply_reduce_fusion.2
  793.0 1.5 convolution_add_fusion.2
  796.7 2.0 multiply_reduce_fusion.2
  799.4 1.5 convolution_add_fusion.2
  802.4 112.9 %psum.63 = f32[]{:T(128)} all-reduce(f32[]{:T(128)} %get-tuple-element.408), channel_id=1, replica_groups=mesh['batch'=32,'proto'=16] {'batch','proto'}, use_global_device_ids=true, to_apply=%region_18.19 | all-reduce | flops 1 | bytes 8 | tf_op jit(solution)/shard_map/psum | solution.py:111
  916.0 27.3 %all-reduce.2.cloned.1.call-done = f32[128,256]{1,0:T(8,128)} async-done(((f32[128,256]{1,0:T(8,128)}), f32[128,256]{1,0:T(8,128)}) %all-reduce.2.cloned.1.call-update) | async-done | bytes 131088 | tf_op jit(solution)/shard_map/psum | solution.py:110
  943.3 1.6 copy.52
  (122 shorter events, 23.3 us)
Async XLA Ops:
  7.2 140.0 %copy-start = (bf16[128,256]{1,0:T(8,128)(2,1)S(1)}, bf16[128,256]{1,0:T(8,128)(2,1)}, u32[]{:S(2)}) copy-start(bf16[128,256]{1,0:T(8,128)(2,1)} %param.10) | copy-start | bytes 196612
  7.2 69.5 %all-gather.9.cloned.1.call-start = ((), (), s32[]{:S(2)}) async-start(), calls=%async_computation.1 | async-start | bytes 4325376 | tf_op jit(solution)/shard_map/all_gather | solution.py:50
  7.9 139.3 %all-gather.7.cloned.1.call-start = ((), (), s32[]{:S(2)}) async-start(), calls=%async_computation | async-start | bytes 4325376 | tf_op jit(solution)/shard_map/all_gather | solution.py:49
  8.7 934.6 %all-reduce.2.cloned.1.call-start = ((), (), s32[]{:S(2)}) async-start(), calls=%async_computation.2 | async-start | bytes 262144 | tf_op jit(solution)/shard_map/psum | solution.py:110
  265.0 2.0 copy-start.1
  592.2 158.7 %copy-start.2 = (bf16[128,256]{1,0:T(8,128)(2,1)S(1)}, bf16[128,256]{1,0:T(8,128)(2,1)}, u32[]{:S(2)}) copy-start(bf16[128,256]{1,0:T(8,128)(2,1)} %get-tuple-element.773) | copy-start | bytes 196612
  801.8 0.7 copy-start.3
Sparse Core Ops, SparseCore 0:
  11.1 65.4 all-gather.8
  79.8 60.8 all-gather.6
  802.6 140.6 all-reduce.1
where the time goes:
time: 954 us; the launch traced here: 953 us
  blocking collectives  736 us (77%)
  waiting for transfers between devices  96.6 us (10%)
  matrix products  70.9 us (7%)
  local copies, waits for them, and re-layouts  22.9 us (2%)
  between operations  15.6 us (2%)
    psum x3, blocking collectives, on_device(): colsum = lax.psum(colsum, 'batch')  371 us
    psum x1, blocking collectives, on_device(): loss_value = lax.psum(loss_part, ('batch', 'proto')) / total_rows  113 us
    pmax x1, blocking collectives, on_device(): lax.pmax(jnp.max(scores, axis=0).astype(jnp.bfloat16), 'batch')  109 us
    psum x3, blocking collectives, on_device(): rowsum = lax.psum(rowsum, 'proto')  85.1 us
    all_gather x1, waiting for transfers between devices, on_device(): lax.all_gather(student_proto, 'batch', axis=0, tiled=True)  67.9 us
    all_gather x2, blocking collectives, merged(): gathered = jax.tree.map(lambda a: lax.all_gather(a, axis), part)  57 us
    dot_general x17, matrix products, map_against_centers(): lax.dot_general(embedding_lines, center_lines, (((1,), (1,)), ((), ())),...  33.1 us
    psum x1, waiting for transfers between devices, on_device(): student_grad = lax.psum(grad_part, 'proto')  27.3 us
  transfers between devices with their start and end apart: 3, of which 2 were waited for; matrix products, arithmetic and copies ran while one was open for 1% of the time, Pallas kernels for 0%

commit v1 on v0

v1 whole, which is shorter than its diff:
```python
import jax
import jax.numpy as jnp
from jax import lax
from jax.experimental import pallas as pl
from jax.experimental.pallas import tpu as pltpu
from jax.sharding import PartitionSpec as P

PROTOS = 131072
ROWS = 4096
TEACHER_TEMP = 0.07
STUDENT_TEMP = 0.1
LOG2E = 1.4426950408889634
KT = LOG2E / TEACHER_TEMP
KS = LOG2E / STUDENT_TEMP
F32 = jnp.float32
BF16 = jnp.bfloat16
NT = (((1,), (1,)), ((), ()))
Z_ORDER = (8, 7, 9, 6, 10, 5, 11, 4, 12, 3, 13, 2, 14, 1, 15)


def across(row):
    return jnp.broadcast_to(row, (128, 128)).T


def lane_sums(a):
    return jnp.sum(a.T, axis=0, keepdims=True)


def twice(a):
    return jnp.concatenate([a, a], axis=1)


def halves(a):
    return a[:, :128] + a[:, 128:]


def product(values, centers):
    high = values.astype(BF16)
    low = (values - high.astype(F32)).astype(BF16)
    return jnp.dot(high, centers, preferred_element_type=F32) + jnp.dot(
        low, centers, preferred_element_type=F32
    )


def kernel(
    tf, sf, tp, sp,
    targets, grad, loss,
    TF, SF, TP, SP, K2, KR, LG, TG,
    MC, CS, FS, CE, ACC, WB,
    C1, CB, RY, RZ, MY, CY, ST, BS, BR, RT, AS, AR, GS, LY, LC,
    local_sem, gather_send, gather_recv, ex_send, ex_recv, out_sem,
):
    b, z = lax.axis_index("batch"), lax.axis_index("proto")
    y, x, c = b // 8, lax.rem(b // 2, 4), lax.rem(b, 2)
    xc = lax.rem(b, 8)

    def at(y_, x_, c_):
        return {"batch": (lax.rem(y_, 4) * 4 + lax.rem(x_, 4)) * 2 + c_}

    sibling = at(y, x, 1 - c)
    y_group = [at(y + i, x, c) for i in (1, 3, 2)]
    xc_group = [{"batch": y * 8 + lax.rem(xc + i, 8)} for i in range(1, 8)]
    z_group = [{"proto": lax.rem(z + i, 16)} for i in Z_ORDER]

    loads = [
        pltpu.make_async_copy(tp, TP.at[c, y, x], local_sem.at[0]),
        pltpu.make_async_copy(tf, TF.at[y], local_sem.at[1]),
        pltpu.make_async_copy(sp, SP.at[c, x, y], local_sem.at[2]),
        pltpu.make_async_copy(sf, SF, local_sem.at[3]),
    ]
    for load in loads:
        load.start()

    barrier = pltpu.get_barrier_semaphore()
    partners = z_group + xc_group + y_group
    for partner in partners:
        pl.semaphore_signal(barrier, inc=1, device_id=partner)
    pl.semaphore_wait(barrier, len(partners))

    unsent = []
    used = [0]

    def send(ref, device, recv_sem, dst=None):
        k = used[0]
        used[0] += 1
        copy = pltpu.make_async_remote_copy(
            src_ref=ref,
            dst_ref=ref if dst is None else dst,
            send_sem=gather_send.at[k],
            recv_sem=recv_sem,
            device_id=device,
        )
        copy.start()
        unsent.append((ref, gather_send.at[k]))

    def arrived(ref, sem):
        pltpu.make_async_copy(ref, ref, sem).wait()

    exchanges = [0]

    def exchange(buf, me, group):
        k = exchanges[0]
        exchanges[0] += 1
        for device in group:
            pltpu.make_async_remote_copy(
                src_ref=buf.at[me],
                dst_ref=buf.at[me],
                send_sem=ex_send.at[k],
                recv_sem=ex_recv.at[k],
                device_id=device,
            ).start()
        all_of = buf.at[pl.ds(0, len(group))]
        unsent.append((all_of, ex_send.at[k]))
        return lambda: arrived(all_of, ex_recv.at[k])

    def scatter(src, buf):
        k = exchanges[0]
        exchanges[0] += 1
        for i in Z_ORDER:
            t = lax.rem(z + i, 16)
            pltpu.make_async_remote_copy(
                src_ref=src.at[t],
                dst_ref=buf.at[z],
                send_sem=ex_send.at[k],
                recv_sem=ex_recv.at[k],
                device_id={"proto": t},
            ).start()
        buf[z] = src[z]
        all_of = buf.at[pl.ds(0, 15)]
        unsent.append((all_of, ex_send.at[k]))
        return lambda: arrived(all_of, ex_recv.at[k])

    loads[0].wait()
    for i in (1, 3, 2):
        send(TP.at[c, y, x], at(y, x + i, c), gather_recv.at[i - 1])
    send(TP.at[c, y, x], sibling, gather_recv.at[3])
    loads[1].wait()
    for i in (1, 3, 2):
        send(TF.at[y], at(y + i, x, c), gather_recv.at[6 + i])
    loads[2].wait()
    for i in (1, 3, 2):
        send(SP.at[c, x, y], at(y + i, x, c), gather_recv.at[9 + i])
    loads[3].wait()

    for i in (1, 3, 2):
        block = TP.at[c, y, lax.rem(x + 4 - i, 4)]
        arrived(block, gather_recv.at[i - 1])
        send(block, sibling, gather_recv.at[3 + i])
    for i in (1, 3, 2):
        send(TP.at[c, y], at(y + i, x, c), gather_recv.at[12 + i])
    for i in (1, 3, 2):
        arrived(TF.at[lax.rem(y + 4 - i, 4)], gather_recv.at[6 + i])

    def score_block(cc, xx):
        j = cc * 4 + xx
        scores = lax.dot_general(
            TF[...].reshape(512, 256), TP[cc, y, xx], NT, preferred_element_type=F32
        )
        K2[j] = scores
        top = jnp.max(scores, axis=0, keepdims=True)
        MC[pl.ds(j, 1), :] = top
        total = jnp.zeros((1, 256), F32)
        for q in range(4):
            e = jnp.exp2((K2[j, q * 128 : q * 128 + 128, :] - top) * KT)
            K2[j, q * 128 : q * 128 + 128, :] = e
            total = total + jnp.sum(e, axis=0, keepdims=True)
        CS[pl.ds(j, 1), :] = total

    @pl.loop(0, 4)
    def _(xx):
        score_block(c, xx)

    for i in range(4):
        arrived(TP.at[1 - c, y, lax.rem(x + 4 - i, 4)], gather_recv.at[3 + i])

    @pl.loop(0, 4)
    def _(xx):
        score_block(1 - c, xx)

    C1[xc, 0] = MC[...]
    C1[xc, 1] = CS[...]
    wait_c1 = exchange(C1, xc, xc_group)
    for i in (1, 3, 2):
        arrived(SP.at[c, x, lax.rem(y + 4 - i, 4)], gather_recv.at[9 + i])
    for i in (1, 3, 2):
        send(SP.at[c, x], at(y, x + i, c), gather_recv.at[15 + i])
    wait_c1()
    top = C1[0, 0]
    for d in range(1, 8):
        top = jnp.maximum(top, C1[d, 0])
    total = jnp.zeros((8, 256), F32)
    for d in range(8):
        total = total + C1[d, 1] * jnp.exp2((C1[d, 0] - top) * KT)
    FS[...] = jnp.exp2((MC[...] - top) * KT)
    MY[y] = top
    wait_my = exchange(MY, y, y_group)
    CE[...] = FS[...] / (PROTOS * total)

    def row_pass(it):
        @pl.loop(0, 8)
        def _(q):
            rows = pl.ds(pl.multiple_of(q * 64, 64), 64)
            acc = jnp.zeros((64, 128), F32)
            for j in range(8):
                acc = acc + halves(K2[j, rows, :] * CE[j : j + 1, :])
            ACC[rows, :] = acc

        for q in range(4):
            RY[it, y, q : q + 1, :] = lane_sums(ACC[q * 128 : q * 128 + 128, :])
        exchange(RY.at[it], y, y_group)()
        r = RY[it, 0]
        for d in range(1, 4):
            r = r + RY[it, d]
        RZ[it, z] = r
        return exchange(RZ.at[it], z, z_group)

    def row_end(it, wait):
        wait()
        r = RZ[it, 0]
        for d in range(1, 16):
            r = r + RZ[it, d]
        w = 1.0 / (ROWS * r)
        for q in range(4):
            WB[q] = across(w[q : q + 1, :])

    def col_pass(it):
        @pl.loop(0, 8)
        def _(j):
            total = jnp.zeros((1, 256), F32)
            for q in range(4):
                part = K2[j, q * 128 : q * 128 + 128, :] * twice(WB[q])
                total = total + jnp.sum(part, axis=0, keepdims=True)
            CS[pl.ds(j, 1), :] = total

        CB[it, xc] = CS[...] * FS[...]
        return exchange(CB.at[it], xc, xc_group)

    def col_end(it, wait):
        wait()
        total = CB[it, 0]
        for d in range(1, 8):
            total = total + CB[it, d]
        return 1.0 / (PROTOS * total)

    wait_row = row_pass(0)
    row_end(0, wait_row)
    col = col_end(0, col_pass(0))
    CE[...] = col * FS[...]
    wait_row = row_pass(1)

    for i in (1, 3, 2):
        part = TP.at[c, lax.rem(y + 4 - i, 4)]
        arrived(part, gather_recv.at[12 + i])
        send(part, sibling, gather_recv.at[18 + i])
    send(SP.at[c, x], sibling, gather_recv.at[22])
    for i in (1, 3, 2):
        part = SP.at[c, lax.rem(x + 4 - i, 4)]
        arrived(part, gather_recv.at[15 + i])
        send(part, sibling, gather_recv.at[22 + i])
    wait_my()

    for i in (1, 3, 2):
        arrived(TP.at[1 - c, lax.rem(y + 4 - i, 4)], gather_recv.at[18 + i])

    def place(g):
        return g // 8, lax.rem(g // 2, 4), lax.rem(g, 2)

    @pl.loop(0, 32)
    def _(g):
        yy, xx, cc = place(g)
        scores = lax.dot_general(TF[y], TP[cc, yy, xx], NT, preferred_element_type=F32)
        KR[g] = jnp.exp2((scores - MY[yy, pl.ds(cc * 4 + xx, 1), :]) * KT)

    row_end(1, wait_row)
    wait_col = col_pass(1)

    for i in range(4):
        arrived(SP.at[1 - c, lax.rem(x + 4 - i, 4)], gather_recv.at[22 + i])

    def logit_block(g, most):
        yy, xx, cc = place(g)
        logits = lax.dot_general(SF[...], SP[cc, xx, yy], NT, preferred_element_type=F32)
        LG[g] = logits
        return jnp.maximum(most, jnp.maximum(logits[:, :128], logits[:, 128:]))

    most = lax.fori_loop(0, 32, logit_block, jnp.full((128, 128), -jnp.inf, F32))
    most = jnp.max(most, axis=1, keepdims=True)

    def softmax_block(g, carried):
        total, out = carried
        yy, xx, cc = place(g)
        below = LG[g] - most
        LG[g] = below
        e = jnp.exp2(below * KS)
        return total + halves(e), out + product(e, SP[cc, xx, yy])

    total, soft = lax.fori_loop(
        0, 32, softmax_block, (jnp.zeros((128, 128), F32), jnp.zeros((128, 256), F32))
    )
    ST[z, 0:1, :] = jnp.broadcast_to(most, (128, 128)).T[0:1, :]
    ST[z, 1:2, :] = lane_sums(total)
    wait_st = exchange(ST, z, z_group)

    CY[y] = col_end(1, wait_col)
    wait_cy = exchange(CY, y, y_group)

    wait_st()
    tops = ST[:, 0, :]
    row_top = jnp.max(tops, axis=0, keepdims=True)
    row_sum = jnp.sum(ST[:, 1, :] * jnp.exp2((tops - row_top) * KS), axis=0, keepdims=True)
    below_top = ST[z, 0:1, :] - row_top
    BS[...] = (soft * twice(across(jnp.exp2(below_top * KS) / row_sum))).reshape(16, 8, 256)
    wait_b = scatter(BS, BR)
    wait_cy()

    def plan_block(g, carried):
        rsum, tsum, out = carried
        yy, xx, cc = place(g)
        share = KR[g] * CY[yy, pl.ds(cc * 4 + xx, 1), :]
        KR[g] = share
        return (
            rsum + halves(share),
            tsum + halves(share * LG[g]),
            out + product(share, SP[cc, xx, yy]),
        )

    rsum, tsum, out = lax.fori_loop(
        0,
        32,
        plan_block,
        (jnp.zeros((128, 128), F32), jnp.zeros((128, 128), F32), jnp.zeros((128, 256), F32)),
    )
    r = lane_sums(rsum)
    RT[z, 0:1, :] = r
    RT[z, 1:2, :] = lane_sums(tsum) + r * below_top
    wait_rt = exchange(RT, z, z_group)
    AS[...] = out.reshape(16, 8, 256)
    wait_a = scatter(AS, AR)

    wait_rt()
    r, t = RT[0, 0:1, :], RT[0, 1:2, :]
    for d in range(1, 16):
        r, t = r + RT[d, 0:1, :], t + RT[d, 1:2, :]
    weight = 1.0 / r
    part = jnp.log(row_sum) - weight * t * (1.0 / STUDENT_TEMP)
    LY[y] = jnp.broadcast_to(part, (8, 128))
    wait_ly = exchange(LY, y, y_group)
    WB[0] = across(weight)

    wait_b()
    wait_a()
    plan_sum, soft_sum = AR[0], BR[0]
    for d in range(1, 16):
        plan_sum, soft_sum = plan_sum + AR[d], soft_sum + BR[d]
    mine = WB[0, pl.ds(pl.multiple_of(z * 8, 8), 8), :]
    GS[z] = (soft_sum - twice(mine) * plan_sum) / (ROWS * STUDENT_TEMP)
    wait_gs = exchange(GS, z, z_group)

    writes = []
    for q in range(4):

        @pl.loop(0, 8)
        def _(n):
            g = q * 8 + n
            columns = pl.ds(pl.multiple_of(g * 256, 256), 256)
            TG[:, columns] = (KR[g] * twice(WB[0])).astype(BF16)

        columns = slice(q * 2048, q * 2048 + 2048)
        write = pltpu.make_async_copy(TG.at[:, columns], targets.at[:, columns], out_sem.at[q])
        write.start()
        writes.append(write)

    wait_ly()
    LC[xc] = ((LY[0] + LY[1]) + LY[2]) + LY[3]
    wait_lc = exchange(LC, xc, xc_group)
    wait_lc()
    part = LC[0]
    for d in range(1, 8):
        part = part + LC[d]
    loss[...] = jnp.sum(part, axis=1, keepdims=True)[0:1, :] / ROWS

    wait_gs()
    grad[...] = GS[...].reshape(128, 256)
    for write in writes:
        write.wait()
    for ref, sem in unsent:
        arrived(ref, sem)


def on_device(teacher_feat, student_feat, teacher_proto, student_proto):
    any_spec = pl.BlockSpec(memory_space=pl.ANY)
    vmem_spec = pl.BlockSpec(memory_space=pltpu.VMEM)

    def f32(*shape):
        return pltpu.VMEM(shape, F32)

    def bf16(*shape):
        return pltpu.VMEM(shape, BF16)

    targets, grad, loss = pl.pallas_call(
        kernel,
        out_shape=(
            jax.ShapeDtypeStruct((128, 8192), BF16),
            jax.ShapeDtypeStruct((128, 256), F32),
            jax.ShapeDtypeStruct((1, 1), F32),
        ),
        in_specs=[any_spec] * 4,
        out_specs=(any_spec, vmem_spec, vmem_spec),
        scratch_shapes=[
            bf16(4, 128, 256),
            bf16(128, 256),
            bf16(2, 4, 4, 256, 256),
            bf16(2, 4, 4, 256, 256),
            f32(8, 512, 256),
            f32(32, 128, 256),
            f32(32, 128, 256),
            bf16(128, 8192),
            f32(8, 256),
            f32(8, 256),
            f32(8, 256),
            f32(8, 256),
            f32(512, 128),
            f32(4, 128, 128),
            f32(8, 2, 8, 256),
            f32(2, 8, 8, 256),
            f32(2, 4, 4, 128),
            f32(2, 16, 4, 128),
            f32(4, 8, 256),
            f32(4, 8, 256),
            f32(16, 2, 128),
            f32(16, 8, 256),
            f32(16, 8, 256),
            f32(16, 2, 128),
            f32(16, 8, 256),
            f32(16, 8, 256),
            f32(16, 8, 256),
            f32(4, 8, 128),
            f32(8, 8, 128),
            pltpu.SemaphoreType.DMA((4,)),
            pltpu.SemaphoreType.DMA((26,)),
            pltpu.SemaphoreType.DMA((26,)),
            pltpu.SemaphoreType.DMA((16,)),
            pltpu.SemaphoreType.DMA((16,)),
            pltpu.SemaphoreType.DMA((4,)),
        ],
        compiler_params=pltpu.CompilerParams(
            collective_id=0, has_side_effects=True, vmem_limit_bytes=48 * 2**20
        ),
        cost_estimate=pl.CostEstimate(
            flops=2_000_000_000, bytes_accessed=4_000_000, transcendentals=4_000_000
        ),
    )(teacher_feat, student_feat, teacher_proto, student_proto)
    return targets, grad, loss[0, 0]


def solution(mesh):
    return jax.shard_map(
        on_device,
        mesh=mesh,
        in_specs=(
            P("batch", None),
            P("batch", None),
            P(("proto", "batch"), None),
            P(("proto", "batch"), None),
        ),
        out_specs=(P("batch", "proto"), P("batch", None), P()),
        check_vma=False,
    )
```

time: 954 us -> 129 us (0.14)
  blocking collectives: 736 us -> 0 us
  Pallas kernels: 0 us -> 120 us
  waiting for transfers between devices: 96.6 us -> 0 us
  matrix products: 70.9 us -> 0 us
  local copies, waits for them, and re-layouts: 22.9 us -> 5.46 us
  between operations: 15.6 us -> 2.4 us
    psum x7 -> x0, blocking collectives: 569 us -> none  [the longest x3 371 us: on_device(): colsum = lax.psum(colsum, 'batch')]
    pallas_call x0 -> x1, Pallas kernels: none -> 120 us  [on_device(): pl.pallas_call(kernel, out_shape=(jax.ShapeDtypeStruct((128, 8192), BF16)...]
    pmax x1 -> x0, blocking collectives: 109 us -> none  [on_device(): lax.pmax(jnp.max(scores, axis=0).astype(jnp.bfloat16), 'batch')]
    dot_general x31 -> x0, matrix products: 70.9 us -> none  [the longest x17 33.1 us: map_against_centers(): lax.dot_general(embedding_lines, center_lines, (((1,), (1,)), ((), ())),...]
    all_gather x2 -> x0, waiting for transfers between devices: 67.9 us -> none  [the longest x1 67.9 us: on_device(): lax.all_gather(student_proto, 'batch', axis=0, tiled=True)]
    all_gather x2 -> x0, blocking collectives: 57 us -> none  [merged(): gathered = jax.tree.map(lambda a: lax.all_gather(a, axis), part)]
    psum x1 -> x0, waiting for transfers between devices: 27.3 us -> none  [on_device(): student_grad = lax.psum(grad_part, 'proto')]
    dynamic_slice x26 -> x0, local copies, waits for them, and re-layouts: 10.1 us -> none  [the longest x16 10.1 us: last_pass(): lax.dynamic_slice_in_dim(kernel, block_index * block_cols, block_cols, 1)]
  transfers between devices with their start and end apart: 3 -> 0, of which waited for: 2 -> 0; matrix products, arithmetic and copies ran while one was open for 1% -> 0% of each run, Pallas kernels for 0% -> 0%
where the time goes in v1:
time: 129 us; the launch traced here: 128 us
  Pallas kernels  120 us (93%)
  local copies, waits for them, and re-layouts  5.46 us (4%)
  between operations  2.4 us (2%)
    pallas_call x1, Pallas kernels, on_device(): pl.pallas_call(kernel, out_shape=(jax.ShapeDtypeStruct((128, 8192), BF16)...  120 us
    unnamed x10, local copies, waits for them, and re-layouts  5.46 us

profile of v1, /device:TPU:6, one launch (start us, length us, event | category | flops | bytes accessed | tf_op | source)
XLA Modules:
  0.0 128.3 jit_solution(12794417150974215258)
XLA Ops:
  0.6 0.0 copy-start
  0.6 0.9 copy-done
  1.5 0.0 copy-start.1
  1.5 0.9 copy-done.1
  2.4 0.0 copy-start.2
  2.4 0.8 copy-done.2
  3.3 0.0 copy-start.3
  3.3 0.8 copy-done.3
  4.1 120.4 %shard_map.67 = (bf16[128,8192]{1,0:T(8,128)(2,1)S(1)}, f32[128,256]{1,0:T(8,128)S(1)}, f32[1,1]{1,0:T(1,128)}) custom-call(bf16[128,256]{1,0:T(8,128)(2,1)S(1)} %copy-done.2, bf16[128,256]{1,0:T(8,128)(2,1)S(1)} %copy-done.3, bf16[256,256]{1,0:T(8,128)(2,1)S(1)} %copy-done, bf16[256,256]{1,0:T(8,128)(2,1)S(1)} %copy-done.1), custom_call_target="tpu_custom_call" | custom-call | flops 2000000000 | bytes 4000000 | tf_op jit(solution)/shard_map/pallas_call | solution.py:400
  124.5 1.3 %copy.10 = bf16[128,8192]{1,0:T(8,128)(2,1)} copy(bf16[128,8192]{1,0:T(8,128)(2,1)S(1)} %get-tuple-element.12) | data formatting | bytes 4194304
  125.9 0.7 copy.11
Async XLA Ops:
  0.6 0.9 copy-start
  1.5 0.9 copy-start.1
  2.4 0.8 copy-start.2
  3.3 0.8 copy-start.3

commit v2 on v1

--- a/solution.py
+++ b/solution.py
@@ -46,7 +46,7 @@
     tf, sf, tp, sp,
     targets, grad, loss,
     TF, SF, TP, SP, K2, KR, LG, TG,
-    MC, CS, FS, CE, ACC, WB,
+    MC, CS, FS, CE, ACC, WB, TOPS, SUMS, SOFT,
     C1, CB, RY, RZ, MY, CY, ST, BS, BR, RT, AS, AR, GS, LY, LC,
     local_sem, gather_send, gather_recv, ex_send, ex_recv, out_sem,
 ):
@@ -147,8 +147,6 @@
         arrived(block, gather_recv.at[i - 1])
         send(block, sibling, gather_recv.at[3 + i])
     for i in (1, 3, 2):
-        send(TP.at[c, y], at(y + i, x, c), gather_recv.at[12 + i])
-    for i in (1, 3, 2):
         arrived(TF.at[lax.rem(y + 4 - i, 4)], gather_recv.at[6 + i])
 
     def score_block(cc, xx):
@@ -182,9 +180,10 @@
     wait_c1 = exchange(C1, xc, xc_group)
     for i in (1, 3, 2):
         arrived(SP.at[c, x, lax.rem(y + 4 - i, 4)], gather_recv.at[9 + i])
-    for i in (1, 3, 2):
-        send(SP.at[c, x], at(y, x + i, c), gather_recv.at[15 + i])
     wait_c1()
+    send(SP.at[c, x, pl.ds(0, 3)], at(y, x + 1, c), gather_recv.at[13])
+    send(SP.at[c, x, pl.ds(0, 3)], at(y, x + 3, c), gather_recv.at[14])
+    send(SP.at[c, x], sibling, gather_recv.at[15])
     top = C1[0, 0]
     for d in range(1, 8):
         top = jnp.maximum(top, C1[d, 0])
@@ -242,76 +241,115 @@
             total = total + CB[it, d]
         return 1.0 / (PROTOS * total)
 
+    x_less, x_more, x_far = lax.rem(x + 3, 4), lax.rem(x + 1, 4), lax.rem(x + 2, 4)
+    y_less, y_more, y_far = lax.rem(y + 3, 4), lax.rem(y + 1, 4), lax.rem(y + 2, 4)
+    low, high = pl.ds(0, 2), pl.ds(2, 2)
+
+    def kernel_rows(yy):
+        @pl.loop(0, 8)
+        def _(j):
+            cc, xx = j // 4, lax.rem(j, 4)
+            scores = lax.dot_general(TF[y], TP[cc, yy, xx], NT, preferred_element_type=F32)
+            KR[(yy * 4 + xx) * 2 + cc] = jnp.exp2((scores - MY[yy, pl.ds(j, 1), :]) * KT)
+
+    def softmax_part(xs):
+        old = TOPS[...]
+        top = old
+        for xx in xs:
+
+            def logit_block(n, top, xx=xx):
+                cc, yy = n // 4, lax.rem(n, 4)
+                logits = lax.dot_general(SF[...], SP[cc, xx, yy], NT, preferred_element_type=F32)
+                LG[(yy * 4 + xx) * 2 + cc] = logits
+                return jnp.maximum(top, jnp.maximum(logits[:, :128], logits[:, 128:]))
+
+            top = lax.fori_loop(0, 8, logit_block, top)
+        top = jnp.broadcast_to(jnp.max(top, axis=1, keepdims=True), (128, 128))
+        shrink = jnp.exp2((old - top) * KS)
+        TOPS[...] = top
+        state = SUMS[...] * shrink, SOFT[...] * twice(shrink)
+        for xx in xs:
+
+            def softmax_block(n, carried, xx=xx):
+                total, out = carried
+                cc, yy = n // 4, lax.rem(n, 4)
+                e = jnp.exp2((LG[(yy * 4 + xx) * 2 + cc] - twice(TOPS[...])) * KS)
+                return total + halves(e), out + product(e, SP[cc, xx, yy])
+
+            state = lax.fori_loop(0, 8, softmax_block, state)
+        SUMS[...], SOFT[...] = state
+
+    TOPS[...] = jnp.full((128, 128), -jnp.inf, F32)
+    SUMS[...] = jnp.zeros((128, 128), F32)
+    SOFT[...] = jnp.zeros((128, 256), F32)
+
     wait_row = row_pass(0)
+    send(TP.at[c, y], at(y + 1, x, c), gather_recv.at[16])
+    send(TP.at[c, y], at(y + 3, x, c), gather_recv.at[17])
+    kernel_rows(y)
+    arrived(SP.at[1 - c, x], gather_recv.at[15])
+    softmax_part((x,))
     row_end(0, wait_row)
     col = col_end(0, col_pass(0))
     CE[...] = col * FS[...]
+    arrived(SP.at[c, x_less, pl.ds(0, 3)], gather_recv.at[13])
+    arrived(SP.at[c, x_more, pl.ds(0, 3)], gather_recv.at[14])
+    send(SP.at[c, x, pl.ds(3, 1)], at(y, x + 1, c), gather_recv.at[18])
+    send(SP.at[c, x, pl.ds(3, 1)], at(y, x + 3, c), gather_recv.at[19])
+    send(SP.at[c, x_less, low], at(y, x + 1, c), gather_recv.at[20])
+    send(SP.at[c, x_more, pl.ds(2, 1)], at(y, x + 3, c), gather_recv.at[21])
+    send(SP.at[c, x_less, pl.ds(0, 3)], sibling, gather_recv.at[22])
+    send(SP.at[c, x_more, pl.ds(0, 3)], sibling, gather_recv.at[23])
+
     wait_row = row_pass(1)
-
-    for i in (1, 3, 2):
-        part = TP.at[c, lax.rem(y + 4 - i, 4)]
-        arrived(part, gather_recv.at[12 + i])
-        send(part, sibling, gather_recv.at[18 + i])
-    send(SP.at[c, x], sibling, gather_recv.at[22])
-    for i in (1, 3, 2):
-        part = SP.at[c, lax.rem(x + 4 - i, 4)]
-        arrived(part, gather_recv.at[15 + i])
-        send(part, sibling, gather_recv.at[22 + i])
+    arrived(TP.at[c, y_less], gather_recv.at[16])
+    arrived(TP.at[c, y_more], gather_recv.at[17])
+    send(TP.at[c, y_less, low], at(y + 1, x, c), gather_recv.at[24])
+    send(TP.at[c, y_more, high], at(y + 3, x, c), gather_recv.at[25])
+    arrived(SP.at[c, x_less, pl.ds(3, 1)], gather_recv.at[18])
+    arrived(SP.at[c, x_more, pl.ds(3, 1)], gather_recv.at[19])
+    send(SP.at[c, x_more, pl.ds(3, 1)], at(y, x + 3, c), gather_recv.at[26])
+    send(SP.at[c, x_less, pl.ds(3, 1)], sibling, gather_recv.at[27])
+    send(SP.at[c, x_more, pl.ds(3, 1)], sibling, gather_recv.at[28])
+    send(TP.at[c, y_less], sibling, gather_recv.at[29])
+    send(TP.at[c, y_more], sibling, gather_recv.at[30])
+    arrived(SP.at[1 - c, x_less, pl.ds(0, 3)], gather_recv.at[22])
+    arrived(SP.at[1 - c, x_more, pl.ds(0, 3)], gather_recv.at[23])
+    arrived(SP.at[1 - c, x_less, pl.ds(3, 1)], gather_recv.at[27])
+    arrived(SP.at[1 - c, x_more, pl.ds(3, 1)], gather_recv.at[28])
+    softmax_part((x_less, x_more))
+    row_end(1, wait_row)
+    wait_col = col_pass(1)
+
+    arrived(SP.at[c, x_far, low], gather_recv.at[20])
+    arrived(SP.at[c, x_far, pl.ds(2, 1)], gather_recv.at[21])
+    arrived(SP.at[c, x_far, pl.ds(3, 1)], gather_recv.at[26])
+    send(SP.at[c, x_far], sibling, gather_recv.at[31])
+    arrived(TP.at[c, y_far, low], gather_recv.at[24])
+    arrived(TP.at[c, y_far, high], gather_recv.at[25])
+    send(TP.at[c, y_far], sibling, gather_recv.at[32])
     wait_my()
-
-    for i in (1, 3, 2):
-        arrived(TP.at[1 - c, lax.rem(y + 4 - i, 4)], gather_recv.at[18 + i])
+    arrived(TP.at[1 - c, y_less], gather_recv.at[29])
+    arrived(TP.at[1 - c, y_more], gather_recv.at[30])
+    kernel_rows(y_less)
+    kernel_rows(y_more)
+
+    CY[y] = col_end(1, wait_col)
+    wait_cy = exchange(CY, y, y_group)
+
+    arrived(SP.at[1 - c, x_far], gather_recv.at[31])
+    softmax_part((x_far,))
+    ST[z, 0:1, :] = TOPS[...].T[0:1, :]
+    ST[z, 1:2, :] = lane_sums(SUMS[...])
+    wait_st = exchange(ST, z, z_group)
+    BS[...] = SOFT[...].reshape(16, 8, 256)
+    wait_b = scatter(BS, BR)
+    arrived(TP.at[1 - c, y_far], gather_recv.at[32])
+    kernel_rows(y_far)
+    wait_cy()
 
     def place(g):
         return g // 8, lax.rem(g // 2, 4), lax.rem(g, 2)
-
-    @pl.loop(0, 32)
-    def _(g):
-        yy, xx, cc = place(g)
-        scores = lax.dot_general(TF[y], TP[cc, yy, xx], NT, preferred_element_type=F32)
-        KR[g] = jnp.exp2((scores - MY[yy, pl.ds(cc * 4 + xx, 1), :]) * KT)
-
-    row_end(1, wait_row)
-    wait_col = col_pass(1)
-
-    for i in range(4):
-        arrived(SP.at[1 - c, lax.rem(x + 4 - i, 4)], gather_recv.at[22 + i])
-
-    def logit_block(g, most):
-        yy, xx, cc = place(g)
-        logits = lax.dot_general(SF[...], SP[cc, xx, yy], NT, preferred_element_type=F32)
-        LG[g] = logits
-        return jnp.maximum(most, jnp.maximum(logits[:, :128], logits[:, 128:]))
-
-    most = lax.fori_loop(0, 32, logit_block, jnp.full((128, 128), -jnp.inf, F32))
-    most = jnp.max(most, axis=1, keepdims=True)
-
-    def softmax_block(g, carried):
-        total, out = carried
-        yy, xx, cc = place(g)
-        below = LG[g] - most
-        LG[g] = below
-        e = jnp.exp2(below * KS)
-        return total + halves(e), out + product(e, SP[cc, xx, yy])
-
-    total, soft = lax.fori_loop(
-        0, 32, softmax_block, (jnp.zeros((128, 128), F32), jnp.zeros((128, 256), F32))
-    )
-    ST[z, 0:1, :] = jnp.broadcast_to(most, (128, 128)).T[0:1, :]
-    ST[z, 1:2, :] = lane_sums(total)
-    wait_st = exchange(ST, z, z_group)
-
-    CY[y] = col_end(1, wait_col)
-    wait_cy = exchange(CY, y, y_group)
-
-    wait_st()
-    tops = ST[:, 0, :]
-    row_top = jnp.max(tops, axis=0, keepdims=True)
-    row_sum = jnp.sum(ST[:, 1, :] * jnp.exp2((tops - row_top) * KS), axis=0, keepdims=True)
-    below_top = ST[z, 0:1, :] - row_top
-    BS[...] = (soft * twice(across(jnp.exp2(below_top * KS) / row_sum))).reshape(16, 8, 256)
-    wait_b = scatter(BS, BR)
-    wait_cy()
 
     def plan_block(g, carried):
         rsum, tsum, out = carried
@@ -320,7 +358,7 @@
         KR[g] = share
         return (
             rsum + halves(share),
-            tsum + halves(share * LG[g]),
+            tsum + halves(share * (LG[g] - twice(TOPS[...]))),
             out + product(share, SP[cc, xx, yy]),
         )
 
@@ -330,30 +368,40 @@
         plan_block,
         (jnp.zeros((128, 128), F32), jnp.zeros((128, 128), F32), jnp.zeros((128, 256), F32)),
     )
-    r = lane_sums(rsum)
-    RT[z, 0:1, :] = r
-    RT[z, 1:2, :] = lane_sums(tsum) + r * below_top
+    RT[z, 0:1, :] = lane_sums(rsum)
+    RT[z, 1:2, :] = lane_sums(tsum)
     wait_rt = exchange(RT, z, z_group)
     AS[...] = out.reshape(16, 8, 256)
     wait_a = scatter(AS, AR)
 
+    wait_st()
+    tops = ST[:, 0, :]
+    row_top = jnp.max(tops, axis=0, keepdims=True)
+    below = tops - row_top
+    scale = jnp.exp2(below * KS)
+    row_sum = jnp.sum(ST[:, 1, :] * scale, axis=0, keepdims=True)
+    WB[1, :, 0:16] = (scale / row_sum).T
     wait_rt()
-    r, t = RT[0, 0:1, :], RT[0, 1:2, :]
-    for d in range(1, 16):
-        r, t = r + RT[d, 0:1, :], t + RT[d, 1:2, :]
+    r = jnp.sum(RT[:, 0, :], axis=0, keepdims=True)
+    t = jnp.sum(RT[:, 1, :] + RT[:, 0, :] * below, axis=0, keepdims=True)
     weight = 1.0 / r
     part = jnp.log(row_sum) - weight * t * (1.0 / STUDENT_TEMP)
     LY[y] = jnp.broadcast_to(part, (8, 128))
     wait_ly = exchange(LY, y, y_group)
     WB[0] = across(weight)
 
+    mine = pl.ds(pl.multiple_of(z * 8, 8), 8)
     wait_b()
+    scale = WB[1, mine, :]
+    soft_sum = BR[0] * scale[:, 0:1]
+    for d in range(1, 16):
+        soft_sum = soft_sum + BR[d] * scale[:, d : d + 1]
     wait_a()
-    plan_sum, soft_sum = AR[0], BR[0]
+    plan_sum = AR[0]
     for d in range(1, 16):
-        plan_sum, soft_sum = plan_sum + AR[d], soft_sum + BR[d]
-    mine = WB[0, pl.ds(pl.multiple_of(z * 8, 8), 8), :]
-    GS[z] = (soft_sum - twice(mine) * plan_sum) / (ROWS * STUDENT_TEMP)
+        plan_sum = plan_sum + AR[d]
+    mixed = (soft_sum - twice(WB[0, mine, :]) * plan_sum) / (ROWS * STUDENT_TEMP)
+    GS[z] = jnp.concatenate([mixed[:, :128], mixed[:, 128:]], axis=0).astype(BF16)
     wait_gs = exchange(GS, z, z_group)
 
     writes = []
@@ -380,7 +428,10 @@
     loss[...] = jnp.sum(part, axis=1, keepdims=True)[0:1, :] / ROWS
 
     wait_gs()
-    grad[...] = GS[...].reshape(128, 256)
+    for d in range(16):
+        rows = GS[d].astype(F32)
+        grad[d * 8 : d * 8 + 8, :128] = rows[:8]
+        grad[d * 8 : d * 8 + 8, 128:] = rows[8:]
     for write in writes:
         write.wait()
     for ref, sem in unsent:
@@ -397,6 +448,10 @@
     def bf16(*shape):
         return pltpu.VMEM(shape, BF16)
 
+    held = [
+        pltpu.with_memory_space_constraint(a, pltpu.HBM)
+        for a in (teacher_feat, student_feat, teacher_proto, student_proto)
+    ]
     targets, grad, loss = pl.pallas_call(
         kernel,
         out_shape=(
@@ -404,7 +459,7 @@
             jax.ShapeDtypeStruct((128, 256), F32),
             jax.ShapeDtypeStruct((1, 1), F32),
         ),
-        in_specs=[any_spec] * 4,
+        in_specs=[pl.BlockSpec(memory_space=pltpu.HBM)] * 4,
         out_specs=(any_spec, vmem_spec, vmem_spec),
         scratch_shapes=[
             bf16(4, 128, 256),
@@ -421,6 +476,9 @@
             f32(8, 256),
             f32(512, 128),
             f32(4, 128, 128),
+            f32(128, 128),
+            f32(128, 128),
+            f32(128, 256),
             f32(8, 2, 8, 256),
             f32(2, 8, 8, 256),
             f32(2, 4, 4, 128),
@@ -433,12 +491,12 @@
             f32(16, 2, 128),
             f32(16, 8, 256),
             f32(16, 8, 256),
-            f32(16, 8, 256),
+            bf16(16, 16, 128),
             f32(4, 8, 128),
             f32(8, 8, 128),
             pltpu.SemaphoreType.DMA((4,)),
-            pltpu.SemaphoreType.DMA((26,)),
-            pltpu.SemaphoreType.DMA((26,)),
+            pltpu.SemaphoreType.DMA((40,)),
+            pltpu.SemaphoreType.DMA((40,)),
             pltpu.SemaphoreType.DMA((16,)),
             pltpu.SemaphoreType.DMA((16,)),
             pltpu.SemaphoreType.DMA((4,)),
@@ -449,8 +507,8 @@
         cost_estimate=pl.CostEstimate(
             flops=2_000_000_000, bytes_accessed=4_000_000, transcendentals=4_000_000
         ),
-    )(teacher_feat, student_feat, teacher_proto, student_proto)
-    return targets, grad, loss[0, 0]
+    )(*held)
+    return targets, grad, loss.reshape(())
 
 
 def solution(mesh):

time: 129 us -> 97.8 us (0.76)
  Pallas kernels: 120 us -> 92.2 us
  local copies, waits for them, and re-layouts: 5.46 us -> 1.98 us
    pallas_call x1, Pallas kernels: 120 us -> 92.2 us  [on_device(): pl.pallas_call(kernel, out_shape=(jax.ShapeDtypeStruct((128, 8192), BF16)...]
    unnamed x10 -> x2, local copies, waits for them, and re-layouts: 5.46 us -> 1.98 us
where the time goes in v2:
time: 97.8 us; the launch traced here: 96.5 us
  Pallas kernels  92.2 us (94%)
  between operations  2.33 us (2%)
  local copies, waits for them, and re-layouts  1.98 us (2%)
    pallas_call x1, Pallas kernels, on_device(): pl.pallas_call(kernel, out_shape=(jax.ShapeDtypeStruct((128, 8192), BF16)...  92.2 us
    unnamed x2, local copies, waits for them, and re-layouts  1.98 us

profile of v2, /device:TPU:6, one launch (start us, length us, event | category | flops | bytes accessed | tf_op | source)
XLA Modules:
  0.0 96.5 jit_solution(12064830227736888970)
XLA Ops:
  0.6 92.2 %shard_map.67 = (bf16[128,8192]{1,0:T(8,128)(2,1)S(1)}, f32[128,256]{1,0:T(8,128)S(1)}, f32[1,1]{1,0:T(1,128)}) custom-call(bf16[128,256]{1,0:T(8,128)(2,1)} %tf.1, bf16[128,256]{1,0:T(8,128)(2,1)} %sf.1, bf16[256,256]{1,0:T(8,128)(2,1)} %tp.1, bf16[256,256]{1,0:T(8,128)(2,1)} %sp.1), custom_call_target="tpu_custom_call" | custom-call | flops 2000000000 | bytes 4000000 | tf_op jit(solution)/shard_map/pallas_call | solution.py:455
  92.8 1.3 %copy.10 = bf16[128,8192]{1,0:T(8,128)(2,1)} copy(bf16[128,8192]{1,0:T(8,128)(2,1)S(1)} %get-tuple-element.12) | data formatting | bytes 4194304
  94.2 0.7 copy.11

commit v3 on v2

--- a/solution.py
+++ b/solution.py
@@ -48,7 +48,7 @@
     TF, SF, TP, SP, K2, KR, LG, TG,
     MC, CS, FS, CE, ACC, WB, TOPS, SUMS, SOFT,
     C1, CB, RY, RZ, MY, CY, ST, BS, BR, RT, AS, AR, GS, LY, LC,
-    local_sem, gather_send, gather_recv, ex_send, ex_recv, out_sem,
+    relay_sem, local_sem, gather_send, gather_recv, ex_send, ex_recv, out_sem,
 ):
     b, z = lax.axis_index("batch"), lax.axis_index("proto")
     y, x, c = b // 8, lax.rem(b // 2, 4), lax.rem(b, 2)
@@ -57,25 +57,34 @@
     def at(y_, x_, c_):
         return {"batch": (lax.rem(y_, 4) * 4 + lax.rem(x_, 4)) * 2 + c_}
 
+    def around(i):
+        return {"proto": lax.rem(z + i, 16)}
+
     sibling = at(y, x, 1 - c)
     y_group = [at(y + i, x, c) for i in (1, 3, 2)]
     xc_group = [{"batch": y * 8 + lax.rem(xc + i, 8)} for i in range(1, 8)]
-    z_group = [{"proto": lax.rem(z + i, 16)} for i in Z_ORDER]
+    z_group = [around(i) for i in Z_ORDER]
 
     loads = [
         pltpu.make_async_copy(tp, TP.at[c, y, x], local_sem.at[0]),
         pltpu.make_async_copy(tf, TF.at[y], local_sem.at[1]),
-        pltpu.make_async_copy(sp, SP.at[c, x, y], local_sem.at[2]),
+        pltpu.make_async_copy(sp, SP.at[c, y, x], local_sem.at[2]),
         pltpu.make_async_copy(sf, SF, local_sem.at[3]),
     ]
     for load in loads:
         load.start()
 
     barrier = pltpu.get_barrier_semaphore()
-    partners = z_group + xc_group + y_group
+    partners = [around(1), around(15)] + xc_group + y_group
     for partner in partners:
         pl.semaphore_signal(barrier, inc=1, device_id=partner)
     pl.semaphore_wait(barrier, len(partners))
+
+    def announce(k, i):
+        for step in (i, 16 - i):
+            pl.semaphore_signal(relay_sem.at[k], inc=1, device_id=around(step))
+
+    announce(0, 1)
 
     unsent = []
     used = [0]
@@ -130,24 +139,33 @@
         unsent.append((all_of, ex_send.at[k]))
         return lambda: arrived(all_of, ex_recv.at[k])
 
+    x_less, x_more = lax.rem(x + 3, 4), lax.rem(x + 1, 4)
+    y_less, y_more, y_far = lax.rem(y + 3, 4), lax.rem(y + 1, 4), lax.rem(y + 2, 4)
+    y_others = (y_less, y_more, y_far)
+    low, high = pl.ds(0, 2), pl.ds(2, 2)
+    up, down = at(y + 1, x, c), at(y + 3, x, c)
+    right, left = at(y, x + 1, c), at(y, x + 3, c)
+
     loads[0].wait()
     for i in (1, 3, 2):
         send(TP.at[c, y, x], at(y, x + i, c), gather_recv.at[i - 1])
     send(TP.at[c, y, x], sibling, gather_recv.at[3])
     loads[1].wait()
     for i in (1, 3, 2):
-        send(TF.at[y], at(y + i, x, c), gather_recv.at[6 + i])
+        send(TF.at[y], at(y + i, x, c), gather_recv.at[3 + i])
+    for i in (1, 3, 2):
+        send(TP.at[c, y, x], at(y + i, x, c), gather_recv.at[6 + i])
     loads[2].wait()
-    for i in (1, 3, 2):
-        send(SP.at[c, x, y], at(y + i, x, c), gather_recv.at[9 + i])
+    for i in (1, 3):
+        send(SP.at[c, y, x], at(y, x + i, c), gather_recv.at[9 + i])
     loads[3].wait()
 
     for i in (1, 3, 2):
         block = TP.at[c, y, lax.rem(x + 4 - i, 4)]
         arrived(block, gather_recv.at[i - 1])
-        send(block, sibling, gather_recv.at[3 + i])
-    for i in (1, 3, 2):
-        arrived(TF.at[lax.rem(y + 4 - i, 4)], gather_recv.at[6 + i])
+        send(block, sibling, gather_recv.at[12 + i])
+    for i in (1, 3, 2):
+        arrived(TF.at[lax.rem(y + 4 - i, 4)], gather_recv.at[3 + i])
 
     def score_block(cc, xx):
         j = cc * 4 + xx
@@ -168,8 +186,12 @@
     def _(xx):
         score_block(c, xx)
 
-    for i in range(4):
-        arrived(TP.at[1 - c, y, lax.rem(x + 4 - i, 4)], gather_recv.at[3 + i])
+    pl.semaphore_wait(relay_sem.at[0], 2)
+    announce(1, 2)
+
+    arrived(TP.at[1 - c, y, x], gather_recv.at[3])
+    for i in (1, 3, 2):
+        arrived(TP.at[1 - c, y, lax.rem(x + 4 - i, 4)], gather_recv.at[12 + i])
 
     @pl.loop(0, 4)
     def _(xx):
@@ -178,12 +200,15 @@
     C1[xc, 0] = MC[...]
     C1[xc, 1] = CS[...]
     wait_c1 = exchange(C1, xc, xc_group)
-    for i in (1, 3, 2):
-        arrived(SP.at[c, x, lax.rem(y + 4 - i, 4)], gather_recv.at[9 + i])
+    send(SP.at[c, y, x], at(y, x + 2, c), gather_recv.at[11])
+    pl.semaphore_wait(relay_sem.at[1], 2)
+    announce(2, 4)
     wait_c1()
-    send(SP.at[c, x, pl.ds(0, 3)], at(y, x + 1, c), gather_recv.at[13])
-    send(SP.at[c, x, pl.ds(0, 3)], at(y, x + 3, c), gather_recv.at[14])
-    send(SP.at[c, x], sibling, gather_recv.at[15])
+    for i in (1, 3, 2):
+        arrived(TP.at[c, lax.rem(y + 4 - i, 4), x], gather_recv.at[6 + i])
+    for k, yy in enumerate(y_others):
+        send(TP.at[c, yy, x], right, gather_recv.at[17 + k])
+        send(TP.at[c, yy, x], left, gather_recv.at[20 + k])
     top = C1[0, 0]
     for d in range(1, 8):
         top = jnp.maximum(top, C1[d, 0])
@@ -211,6 +236,8 @@
         for d in range(1, 4):
             r = r + RY[it, d]
         RZ[it, z] = r
+        if it == 0:
+            pl.semaphore_wait(relay_sem.at[2], 2)
         return exchange(RZ.at[it], z, z_group)
 
     def row_end(it, wait):
@@ -241,9 +268,7 @@
             total = total + CB[it, d]
         return 1.0 / (PROTOS * total)
 
-    x_less, x_more, x_far = lax.rem(x + 3, 4), lax.rem(x + 1, 4), lax.rem(x + 2, 4)
-    y_less, y_more, y_far = lax.rem(y + 3, 4), lax.rem(y + 1, 4), lax.rem(y + 2, 4)
-    low, high = pl.ds(0, 2), pl.ds(2, 2)
+    x_far = lax.rem(x + 2, 4)
 
     def kernel_rows(yy):
         @pl.loop(0, 8)
@@ -252,31 +277,29 @@
             scores = lax.dot_general(TF[y], TP[cc, yy, xx], NT, preferred_element_type=F32)
             KR[(yy * 4 + xx) * 2 + cc] = jnp.exp2((scores - MY[yy, pl.ds(j, 1), :]) * KT)
 
-    def softmax_part(xs):
+    def softmax_part(parts):
         old = TOPS[...]
         top = old
-        for xx in xs:
-
-            def logit_block(n, top, xx=xx):
-                cc, yy = n // 4, lax.rem(n, 4)
-                logits = lax.dot_general(SF[...], SP[cc, xx, yy], NT, preferred_element_type=F32)
+        for cc, yy in parts:
+
+            def logit_block(xx, top, cc=cc, yy=yy):
+                logits = lax.dot_general(SF[...], SP[cc, yy, xx], NT, preferred_element_type=F32)
                 LG[(yy * 4 + xx) * 2 + cc] = logits
                 return jnp.maximum(top, jnp.maximum(logits[:, :128], logits[:, 128:]))
 
-            top = lax.fori_loop(0, 8, logit_block, top)
+            top = lax.fori_loop(0, 4, logit_block, top)
         top = jnp.broadcast_to(jnp.max(top, axis=1, keepdims=True), (128, 128))
         shrink = jnp.exp2((old - top) * KS)
         TOPS[...] = top
         state = SUMS[...] * shrink, SOFT[...] * twice(shrink)
-        for xx in xs:
-
-            def softmax_block(n, carried, xx=xx):
+        for cc, yy in parts:
+
+            def softmax_block(xx, carried, cc=cc, yy=yy):
                 total, out = carried
-                cc, yy = n // 4, lax.rem(n, 4)
                 e = jnp.exp2((LG[(yy * 4 + xx) * 2 + cc] - twice(TOPS[...])) * KS)
-                return total + halves(e), out + product(e, SP[cc, xx, yy])
-
-            state = lax.fori_loop(0, 8, softmax_block, state)
+                return total + halves(e), out + product(e, SP[cc, yy, xx])
+
+            state = lax.fori_loop(0, 4, softmax_block, state)
         SUMS[...], SOFT[...] = state
 
     TOPS[...] = jnp.full((128, 128), -jnp.inf, F32)
@@ -284,92 +307,89 @@
     SOFT[...] = jnp.zeros((128, 256), F32)
 
     wait_row = row_pass(0)
-    send(TP.at[c, y], at(y + 1, x, c), gather_recv.at[16])
-    send(TP.at[c, y], at(y + 3, x, c), gather_recv.at[17])
+    for i in (1, 3, 2):
+        arrived(SP.at[c, y, lax.rem(x + 4 - i, 4)], gather_recv.at[9 + i])
+    send(SP.at[c, y], up, gather_recv.at[26])
+    send(SP.at[c, y], down, gather_recv.at[27])
+    send(SP.at[c, y], sibling, gather_recv.at[16])
+    for k, yy in enumerate(y_others):
+        send(TP.at[c, yy, x], sibling, gather_recv.at[23 + k])
     kernel_rows(y)
-    arrived(SP.at[1 - c, x], gather_recv.at[15])
-    softmax_part((x,))
+    arrived(SP.at[1 - c, y], gather_recv.at[16])
+    softmax_part(((c, y), (1 - c, y)))
     row_end(0, wait_row)
     col = col_end(0, col_pass(0))
     CE[...] = col * FS[...]
-    arrived(SP.at[c, x_less, pl.ds(0, 3)], gather_recv.at[13])
-    arrived(SP.at[c, x_more, pl.ds(0, 3)], gather_recv.at[14])
-    send(SP.at[c, x, pl.ds(3, 1)], at(y, x + 1, c), gather_recv.at[18])
-    send(SP.at[c, x, pl.ds(3, 1)], at(y, x + 3, c), gather_recv.at[19])
-    send(SP.at[c, x_less, low], at(y, x + 1, c), gather_recv.at[20])
-    send(SP.at[c, x_more, pl.ds(2, 1)], at(y, x + 3, c), gather_recv.at[21])
-    send(SP.at[c, x_less, pl.ds(0, 3)], sibling, gather_recv.at[22])
-    send(SP.at[c, x_more, pl.ds(0, 3)], sibling, gather_recv.at[23])
+    for k, yy in enumerate(y_others):
+        arrived(TP.at[c, yy, x_less], gather_recv.at[17 + k])
+        arrived(TP.at[c, yy, x_more], gather_recv.at[20 + k])
+    for k, yy in enumerate(y_others):
+        send(TP.at[c, yy, x_less, pl.ds(0, 128)], right, gather_recv.at[32 + k])
+        send(TP.at[c, yy, x_more, pl.ds(128, 128)], left, gather_recv.at[35 + k])
 
     wait_row = row_pass(1)
-    arrived(TP.at[c, y_less], gather_recv.at[16])
-    arrived(TP.at[c, y_more], gather_recv.at[17])
-    send(TP.at[c, y_less, low], at(y + 1, x, c), gather_recv.at[24])
-    send(TP.at[c, y_more, high], at(y + 3, x, c), gather_recv.at[25])
-    arrived(SP.at[c, x_less, pl.ds(3, 1)], gather_recv.at[18])
-    arrived(SP.at[c, x_more, pl.ds(3, 1)], gather_recv.at[19])
-    send(SP.at[c, x_more, pl.ds(3, 1)], at(y, x + 3, c), gather_recv.at[26])
-    send(SP.at[c, x_less, pl.ds(3, 1)], sibling, gather_recv.at[27])
-    send(SP.at[c, x_more, pl.ds(3, 1)], sibling, gather_recv.at[28])
-    send(TP.at[c, y_less], sibling, gather_recv.at[29])
-    send(TP.at[c, y_more], sibling, gather_recv.at[30])
-    arrived(SP.at[1 - c, x_less, pl.ds(0, 3)], gather_recv.at[22])
-    arrived(SP.at[1 - c, x_more, pl.ds(0, 3)], gather_recv.at[23])
-    arrived(SP.at[1 - c, x_less, pl.ds(3, 1)], gather_recv.at[27])
-    arrived(SP.at[1 - c, x_more, pl.ds(3, 1)], gather_recv.at[28])
-    softmax_part((x_less, x_more))
+    arrived(SP.at[c, y_less], gather_recv.at[26])
+    arrived(SP.at[c, y_more], gather_recv.at[27])
+    send(SP.at[c, y_less], sibling, gather_recv.at[44])
+    send(SP.at[c, y_more], sibling, gather_recv.at[45])
+    send(SP.at[c, y_less, low], up, gather_recv.at[30])
+    send(SP.at[c, y_more, high], down, gather_recv.at[31])
+    softmax_part([(c, y_less), (c, y_more)])
+    arrived(SP.at[1 - c, y_less], gather_recv.at[44])
+    arrived(SP.at[1 - c, y_more], gather_recv.at[45])
+    for k, yy in enumerate(y_others):
+        send(TP.at[c, yy, x_less], sibling, gather_recv.at[38 + k])
+        send(TP.at[c, yy, x_more], sibling, gather_recv.at[41 + k])
+    softmax_part([(1 - c, y_less), (1 - c, y_more)])
     row_end(1, wait_row)
     wait_col = col_pass(1)
 
-    arrived(SP.at[c, x_far, low], gather_recv.at[20])
-    arrived(SP.at[c, x_far, pl.ds(2, 1)], gather_recv.at[21])
-    arrived(SP.at[c, x_far, pl.ds(3, 1)], gather_recv.at[26])
-    send(SP.at[c, x_far], sibling, gather_recv.at[31])
-    arrived(TP.at[c, y_far, low], gather_recv.at[24])
-    arrived(TP.at[c, y_far, high], gather_recv.at[25])
-    send(TP.at[c, y_far], sibling, gather_recv.at[32])
-    wait_my()
-    arrived(TP.at[1 - c, y_less], gather_recv.at[29])
-    arrived(TP.at[1 - c, y_more], gather_recv.at[30])
-    kernel_rows(y_less)
-    kernel_rows(y_more)
-
-    CY[y] = col_end(1, wait_col)
-    wait_cy = exchange(CY, y, y_group)
-
-    arrived(SP.at[1 - c, x_far], gather_recv.at[31])
-    softmax_part((x_far,))
+    arrived(SP.at[c, y_far, low], gather_recv.at[30])
+    arrived(SP.at[c, y_far, high], gather_recv.at[31])
+    send(SP.at[c, y_far], sibling, gather_recv.at[48])
+    softmax_part([(c, y_far)])
+    for k, yy in enumerate(y_others):
+        arrived(TP.at[c, yy, x_far, pl.ds(0, 128)], gather_recv.at[32 + k])
+        arrived(TP.at[c, yy, x_far, pl.ds(128, 128)], gather_recv.at[35 + k])
+    arrived(SP.at[1 - c, y_far], gather_recv.at[48])
+    for k, yy in enumerate(y_others):
+        send(TP.at[c, yy, x_far], sibling, gather_recv.at[49 + k])
+    softmax_part([(1 - c, y_far)])
     ST[z, 0:1, :] = TOPS[...].T[0:1, :]
     ST[z, 1:2, :] = lane_sums(SUMS[...])
     wait_st = exchange(ST, z, z_group)
     BS[...] = SOFT[...].reshape(16, 8, 256)
     wait_b = scatter(BS, BR)
-    arrived(TP.at[1 - c, y_far], gather_recv.at[32])
-    kernel_rows(y_far)
+
+    CY[y] = col_end(1, wait_col)
+    wait_cy = exchange(CY, y, y_group)
+    wait_my()
+    for k, yy in enumerate(y_others):
+        arrived(TP.at[1 - c, yy, x], gather_recv.at[23 + k])
+        arrived(TP.at[1 - c, yy, x_less], gather_recv.at[38 + k])
+        arrived(TP.at[1 - c, yy, x_more], gather_recv.at[41 + k])
+        arrived(TP.at[1 - c, yy, x_far], gather_recv.at[49 + k])
+    for yy in y_others:
+        kernel_rows(yy)
+
+    def plan_part(yy, carried):
+        def plan_block(j, carried):
+            rsum, out = carried
+            cc, xx = j // 4, lax.rem(j, 4)
+            g = (yy * 4 + xx) * 2 + cc
+            share = KR[g] * CY[yy, pl.ds(j, 1), :]
+            KR[g] = share
+            return rsum + halves(share), out + product(share, SP[cc, yy, xx])
+
+        return lax.fori_loop(0, 8, plan_block, carried)
+
+    state = plan_part(y, (jnp.zeros((128, 128), F32), jnp.zeros((128, 256), F32)))
     wait_cy()
-
-    def place(g):
-        return g // 8, lax.rem(g // 2, 4), lax.rem(g, 2)
-
-    def plan_block(g, carried):
-        rsum, tsum, out = carried
-        yy, xx, cc = place(g)
-        share = KR[g] * CY[yy, pl.ds(cc * 4 + xx, 1), :]
-        KR[g] = share
-        return (
-            rsum + halves(share),
-            tsum + halves(share * (LG[g] - twice(TOPS[...]))),
-            out + product(share, SP[cc, xx, yy]),
-        )
-
-    rsum, tsum, out = lax.fori_loop(
-        0,
-        32,
-        plan_block,
-        (jnp.zeros((128, 128), F32), jnp.zeros((128, 128), F32), jnp.zeros((128, 256), F32)),
-    )
+    for yy in y_others:
+        state = plan_part(yy, state)
+    rsum, out = state
     RT[z, 0:1, :] = lane_sums(rsum)
-    RT[z, 1:2, :] = lane_sums(tsum)
+    RT[z, 1:2, :] = lane_sums(halves(SF[...].astype(F32) * out) - TOPS[...] * rsum)
     wait_rt = exchange(RT, z, z_group)
     AS[...] = out.reshape(16, 8, 256)
     wait_a = scatter(AS, AR)
@@ -494,9 +514,10 @@
             bf16(16, 16, 128),
             f32(4, 8, 128),
             f32(8, 8, 128),
+            pltpu.SemaphoreType.REGULAR((3,)),
             pltpu.SemaphoreType.DMA((4,)),
-            pltpu.SemaphoreType.DMA((40,)),
-            pltpu.SemaphoreType.DMA((40,)),
+            pltpu.SemaphoreType.DMA((56,)),
+            pltpu.SemaphoreType.DMA((56,)),
             pltpu.SemaphoreType.DMA((16,)),
             pltpu.SemaphoreType.DMA((16,)),
             pltpu.SemaphoreType.DMA((4,)),

time: 97.8 us -> 95.7 us (0.979); the launches traced: 96.5 us -> 95.6 us
  no operation moved by 1% of the time
where the time goes in v3:
time: 95.7 us; the launch traced here: 95.6 us
  Pallas kernels  91.3 us (95%)
  between operations  2.33 us (2%)
  local copies, waits for them, and re-layouts  1.98 us (2%)
    pallas_call x1, Pallas kernels, on_device(): pl.pallas_call(kernel, out_shape=(jax.ShapeDtypeStruct((128, 8192), BF16)...  91.3 us
    unnamed x2, local copies, waits for them, and re-layouts  1.98 us

profile of v3, /device:TPU:6, one launch (start us, length us, event | category | flops | bytes accessed | tf_op | source)
XLA Modules:
  0.0 95.6 jit_solution(16083458943852409042)
XLA Ops:
  0.6 91.3 %shard_map.67 = (bf16[128,8192]{1,0:T(8,128)(2,1)S(1)}, f32[128,256]{1,0:T(8,128)S(1)}, f32[1,1]{1,0:T(1,128)}) custom-call(bf16[128,256]{1,0:T(8,128)(2,1)} %tf.1, bf16[128,256]{1,0:T(8,128)(2,1)} %sf.1, bf16[256,256]{1,0:T(8,128)(2,1)} %tp.1, bf16[256,256]{1,0:T(8,128)(2,1)} %sp.1), custom_call_target="tpu_custom_call" | custom-call | flops 2000000000 | bytes 4000000 | tf_op jit(solution)/shard_map/pallas_call | solution.py:475
  91.9 1.3 %copy.10 = bf16[128,8192]{1,0:T(8,128)(2,1)} copy(bf16[128,8192]{1,0:T(8,128)(2,1)S(1)} %get-tuple-element.12) | data formatting | bytes 4194304
  93.2 0.7 copy.11

commit v4 on v3

--- a/solution.py
+++ b/solution.py
@@ -277,6 +277,14 @@
             scores = lax.dot_general(TF[y], TP[cc, yy, xx], NT, preferred_element_type=F32)
             KR[(yy * 4 + xx) * 2 + cc] = jnp.exp2((scores - MY[yy, pl.ds(j, 1), :]) * KT)
 
+    def kernel_column(xx):
+        @pl.loop(0, 6)
+        def _(n):
+            cc, yy = n // 3, lax.rem(y + 1 + lax.rem(n, 3), 4)
+            scores = lax.dot_general(TF[y], TP[cc, yy, xx], NT, preferred_element_type=F32)
+            tops = MY[yy, pl.ds(cc * 4 + xx, 1), :]
+            KR[(yy * 4 + xx) * 2 + cc] = jnp.exp2((scores - tops) * KT)
+
     def softmax_part(parts):
         old = TOPS[...]
         top = old
@@ -317,6 +325,10 @@
     kernel_rows(y)
     arrived(SP.at[1 - c, y], gather_recv.at[16])
     softmax_part(((c, y), (1 - c, y)))
+    wait_my()
+    for k, yy in enumerate(y_others):
+        arrived(TP.at[1 - c, yy, x], gather_recv.at[23 + k])
+    kernel_column(x)
     row_end(0, wait_row)
     col = col_end(0, col_pass(0))
     CE[...] = col * FS[...]
@@ -357,20 +369,18 @@
     softmax_part([(1 - c, y_far)])
     ST[z, 0:1, :] = TOPS[...].T[0:1, :]
     ST[z, 1:2, :] = lane_sums(SUMS[...])
-    wait_st = exchange(ST, z, z_group)
     BS[...] = SOFT[...].reshape(16, 8, 256)
-    wait_b = scatter(BS, BR)
 
     CY[y] = col_end(1, wait_col)
     wait_cy = exchange(CY, y, y_group)
-    wait_my()
-    for k, yy in enumerate(y_others):
-        arrived(TP.at[1 - c, yy, x], gather_recv.at[23 + k])
+    wait_b = scatter(BS, BR)
+    wait_st = exchange(ST, z, z_group)
+    for k, yy in enumerate(y_others):
         arrived(TP.at[1 - c, yy, x_less], gather_recv.at[38 + k])
         arrived(TP.at[1 - c, yy, x_more], gather_recv.at[41 + k])
         arrived(TP.at[1 - c, yy, x_far], gather_recv.at[49 + k])
-    for yy in y_others:
-        kernel_rows(yy)
+    for xx in (x_less, x_more, x_far):
+        kernel_column(xx)
 
     def plan_part(yy, carried):
         def plan_block(j, carried):
@@ -388,11 +398,11 @@
     for yy in y_others:
         state = plan_part(yy, state)
     rsum, out = state
+    AS[...] = out.reshape(16, 8, 256)
+    wait_a = scatter(AS, AR)
     RT[z, 0:1, :] = lane_sums(rsum)
     RT[z, 1:2, :] = lane_sums(halves(SF[...].astype(F32) * out) - TOPS[...] * rsum)
     wait_rt = exchange(RT, z, z_group)
-    AS[...] = out.reshape(16, 8, 256)
-    wait_a = scatter(AS, AR)
 
     wait_st()
     tops = ST[:, 0, :]

time: 95.7 us -> 97.4 us (1.018)
  Pallas kernels: 91.3 us -> 92.3 us
    pallas_call x1, Pallas kernels: 91.3 us -> 92.3 us  [on_device(): pl.pallas_call(kernel, out_shape=(jax.ShapeDtypeStruct((128, 8192), BF16)...]
where the time goes in v4:
time: 97.4 us; the launch traced here: 96.6 us
  Pallas kernels  92.3 us (95%)
  between operations  2.33 us (2%)
  local copies, waits for them, and re-layouts  1.98 us (2%)
    pallas_call x1, Pallas kernels, on_device(): pl.pallas_call(kernel, out_shape=(jax.ShapeDtypeStruct((128, 8192), BF16)...  92.3 us
    unnamed x2, local copies, waits for them, and re-layouts  1.98 us

profile of v4, /device:TPU:6, one launch (start us, length us, event | category | flops | bytes accessed | tf_op | source)
XLA Modules:
  0.0 96.6 jit_solution(2055826880581539467)
XLA Ops:
  0.6 92.3 %shard_map.67 = (bf16[128,8192]{1,0:T(8,128)(2,1)S(1)}, f32[128,256]{1,0:T(8,128)S(1)}, f32[1,1]{1,0:T(1,128)}) custom-call(bf16[128,256]{1,0:T(8,128)(2,1)} %tf.1, bf16[128,256]{1,0:T(8,128)(2,1)} %sf.1, bf16[256,256]{1,0:T(8,128)(2,1)} %tp.1, bf16[256,256]{1,0:T(8,128)(2,1)} %sp.1), custom_call_target="tpu_custom_call" | custom-call | flops 2000000000 | bytes 4000000 | tf_op jit(solution)/shard_map/pallas_call | solution.py:485
  92.9 1.3 %copy.10 = bf16[128,8192]{1,0:T(8,128)(2,1)} copy(bf16[128,8192]{1,0:T(8,128)(2,1)S(1)} %get-tuple-element.12) | data formatting | bytes 4194304
  94.2 0.7 copy.11

commit v5 on v4

--- a/solution.py
+++ b/solution.py
@@ -367,13 +367,13 @@
     for k, yy in enumerate(y_others):
         send(TP.at[c, yy, x_far], sibling, gather_recv.at[49 + k])
     softmax_part([(1 - c, y_far)])
+    BS[...] = SOFT[...].reshape(16, 8, 256)
+    wait_b = scatter(BS, BR)
+
+    CY[y] = col_end(1, wait_col)
+    wait_cy = exchange(CY, y, y_group)
     ST[z, 0:1, :] = TOPS[...].T[0:1, :]
     ST[z, 1:2, :] = lane_sums(SUMS[...])
-    BS[...] = SOFT[...].reshape(16, 8, 256)
-
-    CY[y] = col_end(1, wait_col)
-    wait_cy = exchange(CY, y, y_group)
-    wait_b = scatter(BS, BR)
     wait_st = exchange(ST, z, z_group)
     for k, yy in enumerate(y_others):
         arrived(TP.at[1 - c, yy, x_less], gather_recv.at[38 + k])
@@ -398,11 +398,11 @@
     for yy in y_others:
         state = plan_part(yy, state)
     rsum, out = state
-    AS[...] = out.reshape(16, 8, 256)
-    wait_a = scatter(AS, AR)
     RT[z, 0:1, :] = lane_sums(rsum)
     RT[z, 1:2, :] = lane_sums(halves(SF[...].astype(F32) * out) - TOPS[...] * rsum)
     wait_rt = exchange(RT, z, z_group)
+    AS[...] = out.reshape(16, 8, 256)
+    wait_a = scatter(AS, AR)
 
     wait_st()
     tops = ST[:, 0, :]

time: 97.4 us -> 94.5 us (0.970)
  Pallas kernels: 92.3 us -> 89.9 us
    pallas_call x1, Pallas kernels: 92.3 us -> 89.9 us  [on_device(): pl.pallas_call(kernel, out_shape=(jax.ShapeDtypeStruct((128, 8192), BF16)...]
where the time goes in v5:
time: 94.5 us; the launch traced here: 94.2 us
  Pallas kernels  89.9 us (95%)
  between operations  2.33 us (2%)
  local copies, waits for them, and re-layouts  1.98 us (2%)
    pallas_call x1, Pallas kernels, on_device(): pl.pallas_call(kernel, out_shape=(jax.ShapeDtypeStruct((128, 8192), BF16)...  89.9 us
    unnamed x2, local copies, waits for them, and re-layouts  1.98 us

profile of v5, /device:TPU:6, one launch (start us, length us, event | category | flops | bytes accessed | tf_op | source)
XLA Modules:
  0.0 94.2 jit_solution(15041277142306864651)
XLA Ops:
  0.6 89.9 %shard_map.67 = (bf16[128,8192]{1,0:T(8,128)(2,1)S(1)}, f32[128,256]{1,0:T(8,128)S(1)}, f32[1,1]{1,0:T(1,128)}) custom-call(bf16[128,256]{1,0:T(8,128)(2,1)} %tf.1, bf16[128,256]{1,0:T(8,128)(2,1)} %sf.1, bf16[256,256]{1,0:T(8,128)(2,1)} %tp.1, bf16[256,256]{1,0:T(8,128)(2,1)} %sp.1), custom_call_target="tpu_custom_call" | custom-call | flops 2000000000 | bytes 4000000 | tf_op jit(solution)/shard_map/pallas_call | solution.py:485
  90.5 1.3 %copy.10 = bf16[128,8192]{1,0:T(8,128)(2,1)} copy(bf16[128,8192]{1,0:T(8,128)(2,1)S(1)} %get-tuple-element.12) | data formatting | bytes 4194304
  91.8 0.7 copy.11
